TPU v7x, 32 devices: a whole 2x2x4 slice. The times are simulated.
32 devices in a mesh: seq: 16 (over z, y, core), col: 2 (over x).
Axes of the slice: x: 2, y: 2, z: 4, core: 2. Of those that a mesh axis runs over, the one named last changes fastest.
Arguments:
- memory: bfloat16 [2048, 4096], P('col', 'seq'), may hold values from -8 to 8
- query: bfloat16 [4096, 2048], P('seq', 'col'), may hold values from -400 to 400
- out_grad: bfloat16 [4096, 2048], P('seq', 'col'), may hold values from -96 to 96
- w_key: bfloat16 [4096, 2048], P(None, 'col'), may hold values from -0.09375 to 0.09375
- w_value: bfloat16 [4096, 2048], P(None, 'col'), may hold values from -0.09375 to 0.09375
Outputs:
- d_query: bfloat16 [4096, 2048], P('seq', 'col')
- d_memory: bfloat16 [2048, 4096], P('col', 'seq')
All inputs are finite; a program needn't handle non-finite values.
Results may differ from a plain program's by a relative error of at most 0.02.
The roundings to bfloat16 on the way count: a program that leaves them out, or rounds other values in their place, can miss the bound.
Values may be sent and summed in bfloat16 or wider, within the bound.
No kernel may reach another device: no remote copies, remote signals or barrier semaphores. Data moves between devices by JAX's collectives and lax.ppermute only.
A program may use at most 128 MiB of HBM per device.

v0:
```python
import math

import jax
import jax.numpy as jnp
from jax import lax
from jax.sharding import PartitionSpec as P

HD = 64


def local(memory, query, out_grad, w_key, w_value):
    factor = 1.0 / math.sqrt(HD)
    dealt = lax.all_to_all(memory, "seq", split_axis=0, concat_axis=1, tiled=True)
    mem_local = lax.all_gather(dealt, "col", axis=0, tiled=True)
    key_local = jnp.dot(mem_local, w_key, preferred_element_type=jnp.float32).astype(jnp.bfloat16)
    value_local = jnp.dot(mem_local, w_value, preferred_element_type=jnp.float32).astype(
        jnp.bfloat16
    )
    tgt_rows = query.shape[0]
    local_width = query.shape[1]
    heads_local = local_width // HD
    key_all, value_all = (
        lax.all_gather(key_local, "seq", axis=0, tiled=True),
        lax.all_gather(value_local, "seq", axis=0, tiled=True),
    )
    total_src = key_all.shape[0]
    query_heads = query.reshape(tgt_rows, heads_local, HD)
    grad_heads = out_grad.reshape(tgt_rows, heads_local, HD)
    key_heads = key_all.reshape(total_src, heads_local, HD)
    value_heads = value_all.reshape(total_src, heads_local, HD)
    scores = (
        jnp.einsum("qhd,khd->hqk", query_heads, key_heads, preferred_element_type=jnp.float32)
        * factor
    )
    row_max = jnp.max(scores, axis=-1, keepdims=True)
    expo = jnp.exp(scores - row_max)
    weights = expo / jnp.sum(expo, axis=-1, keepdims=True)
    weights_low = weights.astype(jnp.bfloat16)
    attended = jnp.einsum(
        "hqk,khd->qhd", weights_low, value_heads, preferred_element_type=jnp.float32
    )
    row_delta = jnp.sum(grad_heads.astype(jnp.float32) * attended, axis=-1).T
    prob_grad = jnp.einsum(
        "qhd,khd->hqk", grad_heads, value_heads, preferred_element_type=jnp.float32
    )
    score_grad = (weights * (prob_grad - row_delta[..., None]) * factor).astype(jnp.bfloat16)
    query_grad = jnp.einsum(
        "hqk,khd->qhd", score_grad, key_heads, preferred_element_type=jnp.float32
    )
    d_query = query_grad.reshape(tgt_rows, local_width).astype(jnp.bfloat16)
    key_part = jnp.einsum(
        "hqk,qhd->khd", score_grad, query_heads, preferred_element_type=jnp.float32
    ).reshape(total_src, local_width)
    value_part = jnp.einsum(
        "hqk,qhd->khd", weights_low, grad_heads, preferred_element_type=jnp.float32
    ).reshape(total_src, local_width)
    key_sum, value_sum = (
        lax.psum_scatter(
            key_part.astype(jnp.bfloat16), "seq", scatter_dimension=0, tiled=True
        ).astype(jnp.float32),
        lax.psum_scatter(
            value_part.astype(jnp.bfloat16), "seq", scatter_dimension=0, tiled=True
        ).astype(jnp.float32),
    )
    key_low = key_sum.astype(jnp.bfloat16)
    value_low = value_sum.astype(jnp.bfloat16)
    partial_value = jnp.einsum("ri,di->rd", key_low, w_key, preferred_element_type=jnp.float32)
    partial_value = partial_value + jnp.einsum(
        "ri,di->rd", value_low, w_value, preferred_element_type=jnp.float32
    )
    summed = lax.psum_scatter(
        partial_value.astype(jnp.bfloat16), "col", scatter_dimension=0, tiled=True
    )
    d_memory = lax.all_to_all(summed, "seq", split_axis=1, concat_axis=0, tiled=True)
    return (d_query, d_memory)


def solution(mesh):
    return jax.shard_map(
        local,
        mesh=mesh,
        in_specs=(
            P("col", "seq"),
            P("seq", "col"),
            P("seq", "col"),
            P(None, "col"),
            P(None, "col"),
        ),
        out_specs=(P("seq", "col"), P("col", "seq")),
        check_vma=False,
    )
```

profile of v0, /device:TPU:0, one launch (start us, length us, event | category | flops | bytes accessed | tf_op | source)
XLA Modules:
  0.0 413.6 jit_solution(664578190468319601)
XLA Ops:
  7.2 21.9 %all_to_all.38 = bf16[16,64,256]{2,1,0:T(8,128)(2,1)S(1)} all-to-all(bf16[16,64,256]{2,1,0:T(8,128)(2,1)} %bitcast.87), channel_id=1, replica_groups=mesh['seq'=16,'col'=2] {'seq'}, dimensions={0} | all-to-all | bytes 1048576 | tf_op jit(solution)/shard_map/all_to_all | solution.py:13
  30.0 20.8 %all-gather.4.cloned.1.call-done = bf16[128,4096]{1,0:T(8,128)(2,1)} async-done(((bf16[64,4096]{1,0:T(8,128)(2,1)}), bf16[128,4096]{1,0:T(8,128)(2,1)}) %all-gather.4.cloned.1.call-update) | async-done | bytes 1048592 | tf_op jit(solution)/shard_map/all_gather | solution.py:14
  50.8 5.7 %convolution_convert_fusion.4 = bf16[128,1024]{1,0:T(8,128)(2,1)} fusion(bf16[128,4096]{1,0:T(8,128)(2,1)} %all-gather.4.cloned.1.call-done, bf16[4096,1024]{1,0:T(8,128)(2,1)} %param.8), kind=kOutput, calls=%fused_computation.22 | convolution fusion | flops 1073872896 | bytes 9699328 | tf_op jit(solution)/shard_map/dot_general | solution.py:15
  56.6 5.4 %convolution_convert_fusion.3 = bf16[128,1024]{1,0:T(8,128)(2,1)} fusion(bf16[128,4096]{1,0:T(8,128)(2,1)S(1)} %copy-done.1, bf16[4096,1024]{1,0:T(8,128)(2,1)} %param.9), kind=kOutput, calls=%fused_computation.21 | convolution fusion | flops 1073872896 | bytes 9699328 | tf_op jit(solution)/shard_map/dot_general | solution.py:16
  62.6 44.7 %all-gather.6.cloned.1.call-done = bf16[2048,1024]{1,0:T(8,128)(2,1)} async-done(((bf16[128,1024]{1,0:T(8,128)(2,1)}), bf16[2048,1024]{1,0:T(8,128)(2,1)}) %all-gather.6.cloned.1.call-update) | async-done | bytes 4194320 | tf_op jit(solution)/shard_map/all_gather | solution.py:23
  107.3 6.5 %copy.32 = bf16[2048,1024]{0,1:T(8,128)(2,1)} copy(bf16[2048,1024]{1,0:T(8,128)(2,1)} %all-gather.6.cloned.1.call-done) | data formatting | bytes 8388608 | tf_op jit(solution)/shard_map/all_gather | solution.py:23
  113.8 18.1 %fusion.16 = (f32[16,256]{1,0:T(8,128)S(1)}, f32[16,256,2048]{1,2,0:T(8,128)}) fusion(bf16[2048,16,64]{0,2,1:T(8,128)(2,1)} %bitcast.74, bf16[256,16,64]{0,2,1:T(8,128)(2,1)S(1)} %bitcast.81), kind=kOutput, calls=%fused_computation.25 | convolution fusion | flops 1098909696 | bytes 38289408 | tf_op jit(solution)/shard_map/sub | solution.py:36
  131.9 17.7 %fusion.9 = bf16[16,256,2048]{1,2,0:T(8,128)(2,1)} fusion(f32[16,256,2048]{1,2,0:T(8,128)} %get-tuple-element.9, f32[16,256]{1,0:T(8,128)S(1)} %get-tuple-element.8), kind=kLoop, calls=%fused_computation.11 | loop fusion | flops 16777216 | bytes 50348032 | tf_op jit(solution)/shard_map/convert_element_type | solution.py:38
  149.6 9.5 %all-gather.8.cloned.1.call-done = bf16[2048,1024]{1,0:T(8,128)(2,1)} async-done(((bf16[128,1024]{1,0:T(8,128)(2,1)}), bf16[2048,1024]{1,0:T(8,128)(2,1)}) %all-gather.8.cloned.1.call-update) | async-done | bytes 4194320 | tf_op jit(solution)/shard_map/all_gather | solution.py:24
  159.1 6.5 %copy.34 = bf16[2048,1024]{0,1:T(8,128)(2,1)} copy(bf16[2048,1024]{1,0:T(8,128)(2,1)} %all-gather.8.cloned.1.call-done) | data formatting | bytes 8388608 | tf_op jit(solution)/shard_map/all_gather | solution.py:24
  165.6 10.0 %fusion.14 = f32[256,16]{0,1:T(8,128)S(1)} fusion(bf16[2048,16,64]{0,2,1:T(8,128)(2,1)} %bitcast.76, bf16[16,256,2048]{1,2,0:T(8,128)(2,1)} %fusion.9, bf16[256,16,64]{0,2,1:T(8,128)(2,1)S(1)} %bitcast.78), kind=kOutput, calls=%fused_computation.20 | convolution fusion | flops 1074524160 | bytes 21512192 | tf_op jit(solution)/shard_map/hqk,khd->qhd/dot_general | solution.py:39
  175.7 17.6 %fusion.2 = bf16[16,256,2048]{1,2,0:T(8,128)(2,1)} fusion(bf16[2048,16,64]{0,2,1:T(8,128)(2,1)S(1)} %bitcast.77, bf16[256,16,64]{0,2,1:T(8,128)(2,1)S(1)} %bitcast.79, f32[16,256]{1,0:T(8,128)S(1)} %bitcast.89, f32[16,256,2048]{1,2,0:T(8,128)} %get-tuple-element.9, f32[16,256]{1,0:T(8,128)S(1)} %get-tuple-element.8), kind=kOutput, calls=%fused_computation.3 | convolution fusion | flops 1115684864 | bytes 55083008 | tf_op jit(solution)/shard_map/qhd,khd->hqk/dot_general | solution.py:43
  193.3 10.0 %convolution_convert_fusion.1 = bf16[16,2048,64]{1,2,0:T(8,128)(2,1)} fusion(bf16[16,256,2048]{1,2,0:T(8,128)(2,1)} %fusion.2, bf16[256,16,64]{0,2,1:T(8,128)(2,1)S(1)} %bitcast.82), kind=kOutput, calls=%fused_computation.15 | convolution fusion | flops 1075838976 | bytes 21495808 | tf_op jit(solution)/shard_map/hqk,qhd->khd/dot_general | solution.py:51
  203.3 6.4 %copy.46 = bf16[2048,1024]{1,0:T(8,128)(2,1)} copy(bf16[2048,1024]{0,1:T(8,128)(2,1)} %bitcast.73) | data formatting | bytes 8388608
  209.8 10.0 %convolution_convert_fusion = bf16[16,2048,64]{1,2,0:T(8,128)(2,1)} fusion(bf16[16,256,2048]{1,2,0:T(8,128)(2,1)} %fusion.9, bf16[256,16,64]{0,2,1:T(8,128)(2,1)S(1)} %bitcast.80), kind=kOutput, calls=%fused_computation.14 | convolution fusion | flops 1075838976 | bytes 21495808 | tf_op jit(solution)/shard_map/hqk,qhd->khd/dot_general | solution.py:54
  219.8 6.6 %copy.48 = bf16[2048,1024]{1,0:T(8,128)(2,1)} copy(bf16[2048,1024]{0,1:T(8,128)(2,1)} %bitcast.72) | data formatting | bytes 8388608
  226.5 54.5 %reduce-scatter.10.cloned.1.call-done = bf16[128,1024]{1,0:T(8,128)(2,1)} async-done(((bf16[2048,1024]{1,0:T(8,128)(2,1)}), bf16[128,1024]{1,0:T(8,128)(2,1)}) %reduce-scatter.10.cloned.1.call-update) | async-done | bytes 262160
  281.0 6.3 %fusion.17 = f32[128,4096]{1,0:T(8,128)S(1)} fusion(bf16[128,1024]{1,0:T(8,128)(2,1)} %reduce-scatter.10.cloned.1.call-done, bf16[4096,1024]{1,0:T(8,128)(2,1)} %param.8), kind=kOutput, calls=%fused_computation.26 | convolution fusion | flops 1073741824 | bytes 10747904 | tf_op jit(solution)/shard_map/ri,di->rd/dot_general | solution.py:67
  287.3 69.7 %reduce-scatter.12.cloned.1.call-done = bf16[128,1024]{1,0:T(8,128)(2,1)} async-done(((bf16[2048,1024]{1,0:T(8,128)(2,1)}), bf16[128,1024]{1,0:T(8,128)(2,1)}) %reduce-scatter.12.cloned.1.call-update) | async-done | bytes 262160
  357.0 7.3 %fusion.10 = bf16[128,4096]{1,0:T(8,128)(2,1)} fusion(f32[128,4096]{1,0:T(8,128)S(1)} %fusion.17, bf16[128,1024]{1,0:T(8,128)(2,1)} %reduce-scatter.12.cloned.1.call-done, bf16[4096,1024]{1,0:T(8,128)(2,1)} %param.9), kind=kOutput, calls=%fused_computation.13 | convolution fusion | flops 1074790400 | bytes 11796480 | tf_op jit(solution)/shard_map/ri,di->rd/dot_general | solution.py:68
  364.4 19.6 %reduce-scatter.8.cloned.1.call-done = bf16[64,4096]{1,0:T(8,128)(2,1)} async-done(((bf16[128,4096]{1,0:T(8,128)(2,1)}), bf16[64,4096]{1,0:T(8,128)(2,1)}) %reduce-scatter.8.cloned.1.call-update) | async-done | bytes 524304 | tf_op jit(solution)/shard_map/reduce_scatter | solution.py:71
  385.8 5.6 %all-to-all-start.1 = ((bf16[64,16,256]{2,0,1:T(8,128)(2,1)}), bf16[64,16,256]{2,0,1:T(8,128)(2,1)S(1)}, u32[]{:S(2)}, u32[]{:S(2)}) async-start(bf16[64,16,256]{2,0,1:T(8,128)(2,1)} %bitcast.71), calls=%async_computation.2 | async-start | bytes 1048576 | tf_op jit(solution)/shard_map/all_to_all | solution.py:74
  391.5 9.9 %convolution_convert_fusion.2 = bf16[16,64,256]{2,1,0:T(8,128)(2,1)S(1)} fusion(bf16[2048,16,64]{0,2,1:T(8,128)(2,1)} %bitcast.75, bf16[16,256,2048]{1,2,0:T(8,128)(2,1)} %fusion.2), kind=kOutput, calls=%fused_computation.19 | convolution fusion | flops 1074003968 | bytes 21495808 | tf_op jit(solution)/shard_map/hqk,khd->qhd/dot_general | solution.py:47
  402.3 3.6 all-to-all-done.1
  (26 shorter events, 5.3 us)
Async XLA Ops:
  7.2 43.6 %all-gather.4.cloned.1.call-start = ((), (), s32[]{:S(2)}) async-start(), calls=%async_computation.5 | async-start | bytes 1572864 | tf_op jit(solution)/shard_map/all_gather | solution.py:14
  29.9 77.4 %all-gather.6.cloned.1.call-start = ((), (), s32[]{:S(2)}) async-start(), calls=%async_computation.6 | async-start | bytes 4456448 | tf_op jit(solution)/shard_map/all_gather | solution.py:23
  50.8 5.8 %copy-start.1 = (bf16[128,4096]{1,0:T(8,128)(2,1)S(1)}, bf16[128,4096]{1,0:T(8,128)(2,1)}, u32[]{:S(2)}) copy-start(bf16[128,4096]{1,0:T(8,128)(2,1)} %all-gather.4.cloned.1.call-done) | copy-start | bytes 3145732
  56.5 5.6 %copy-start.2 = (bf16[256,1024]{1,0:T(8,128)(2,1)S(1)}, bf16[256,1024]{1,0:T(8,128)(2,1)}, u32[]{:S(2)}) copy-start(bf16[256,1024]{1,0:T(8,128)(2,1)} %param.6) | copy-start | bytes 1572868
  56.6 5.8 %copy-start.3 = (bf16[256,1024]{1,0:T(8,128)(2,1)S(1)}, bf16[256,1024]{1,0:T(8,128)(2,1)}, u32[]{:S(2)}) copy-start(bf16[256,1024]{1,0:T(8,128)(2,1)} %param.7) | copy-start | bytes 1572868
  56.6 102.5 %all-gather.8.cloned.1.call-start = ((), (), s32[]{:S(2)}) async-start(), calls=%async_computation.7 | async-start | bytes 4456448 | tf_op jit(solution)/shard_map/all_gather | solution.py:24
  62.1 218.9 %reduce-scatter.10.cloned.1.call-start = ((), (), s32[]{:S(2)}) async-start(), calls=%async_computation.9 | async-start | bytes 4456448
  165.6 10.1 %copy-start = (bf16[2048,1024]{0,1:T(8,128)(2,1)S(1)}, bf16[2048,1024]{0,1:T(8,128)(2,1)}, u32[]{:S(2)}) copy-start(bf16[2048,1024]{0,1:T(8,128)(2,1)} %copy.34) | copy-start | bytes 12582916
  209.8 147.3 %reduce-scatter.12.cloned.1.call-start = ((), (), s32[]{:S(2)}) async-start(), calls=%async_computation.10 | async-start | bytes 4456448
  226.4 157.5 %reduce-scatter.8.cloned.1.call-start = ((), (), s32[]{:S(2)}) async-start(), calls=%async_computation.8 | async-start | bytes 1572864 | tf_op jit(solution)/shard_map/reduce_scatter | solution.py:71
  385.8 20.1 %all-to-all-start.1 = ((bf16[64,16,256]{2,0,1:T(8,128)(2,1)}), bf16[64,16,256]{2,0,1:T(8,128)(2,1)S(1)}, u32[]{:S(2)}, u32[]{:S(2)}) async-start(bf16[64,16,256]{2,0,1:T(8,128)(2,1)} %bitcast.71), calls=%async_computation.2 | async-start | bytes 1048576 | tf_op jit(solution)/shard_map/all_to_all | solution.py:74
Sparse Core Ops, SparseCore 0:
  30.0 20.7 all-gather.3
  56.7 50.5 all-gather.5
  110.0 49.0 all-gather.7
  209.9 71.0 reduce-scatter.9
  285.2 71.7 reduce-scatter.11
  364.5 19.4 reduce-scatter.7
where the time goes:
time: 415 us; the launch traced here: 414 us
  waiting for transfers between devices  223 us (54%)
  matrix products  101 us (24%)
  local copies, waits for them, and re-layouts  30.9 us (7%)
  blocking collectives  21.9 us (5%)
  other arithmetic  17.7 us (4%)
  between operations  14.2 us (3%)
  starting transfers between devices  5.86 us (1%)
    unnamed x8, waiting for transfers between devices  124 us
    all_gather x1, waiting for transfers between devices, local(): lax.all_gather(key_local, 'seq', axis=0, tiled=True)  44.7 us
    all_to_all x1, blocking collectives, local(): lax.all_to_all(memory, 'seq', split_axis=0, concat_axis=1, tiled=True)  21.9 us
    all_gather x1, waiting for transfers between devices, local(): mem_local = lax.all_gather(dealt, 'col', axis=0, tiled=True)  20.8 us
    reduce_scatter x1, waiting for transfers between devices, local(): lax.psum_scatter(partial_value.astype(jnp.bfloat16), 'col', scatter_dimen...  19.6 us
    sub x1, matrix products, local(): expo = jnp.exp(scores - row_max)  18.1 us
    convert_element_type x1, other arithmetic, local(): weights_low = weights.astype(jnp.bfloat16)  17.7 us
    dot_general x1, matrix products, local(): jnp.einsum('qhd,khd->hqk', grad_heads, value_heads, preferred_element_typ...  17.6 us
  transfers between devices with their start and end apart: 7, of which 7 were waited for; matrix products, arithmetic and copies ran while one was open for 20% of the time, Pallas kernels for 0%

commit v1 on v0

v1 whole, which is shorter than its diff:
```python
import functools
import math

import jax
import jax.numpy as jnp
from jax import lax
from jax.experimental import pallas as pl
from jax.experimental.pallas import tpu as pltpu
from jax.sharding import PartitionSpec as P

HD = 64
F32 = jnp.float32
BF16 = jnp.bfloat16


def dot(a, b, over_a, over_b):
    return lax.dot_general(
        a, b, (((over_a,), (over_b,)), ((), ())), preferred_element_type=F32
    )


def fold_rows(x, combine):
    return combine(x.reshape(x.shape[0] // 8, 8, x.shape[1]), axis=0)


def attention_kernel(chunk, qg_ref, kv_ref, kt_ref, dq_ref, dkv_ref, s_ref, p_ref, acc_ref):
    step = pl.program_id(1)
    src, tgt = kv_ref.shape[0], qg_ref.shape[0]
    factor = 1.0 / math.sqrt(HD)
    slope = factor * math.log2(math.e)

    @pl.when(step == 0)
    def _():
        acc_ref[...] = jnp.zeros_like(acc_ref)

    qg = qg_ref[...]
    in_query = lax.broadcasted_iota(jnp.int32, qg.shape, 1) < HD
    zero = jnp.zeros_like(qg)
    q_only = jnp.where(in_query, qg, zero)
    g_only = jnp.where(in_query, zero, qg)

    chunks = [pl.ds(at, chunk) for at in range(0, src, chunk)]
    top = None
    for rows in chunks:
        s = dot(kv_ref[rows, :], q_only, 1, 1)
        s_ref[rows, :] = s
        s = fold_rows(s, jnp.max)
        top = s if top is None else jnp.maximum(top, s)
    top = jnp.max(top, axis=0, keepdims=True)

    total = inner = None
    for rows in chunks:
        expo = jnp.exp2((s_ref[rows, :] - top) * slope)
        p = dot(kv_ref[rows, :], g_only, 1, 1)
        s_ref[rows, :] = expo
        p_ref[rows, :] = p
        t, i = fold_rows(expo, jnp.sum), fold_rows(expo * p, jnp.sum)
        total, inner = (t, i) if total is None else (total + t, inner + i)
    inverse = 1.0 / jnp.sum(total, axis=0, keepdims=True)
    delta = jnp.sum(inner, axis=0, keepdims=True) * inverse

    dq = None
    for rows in chunks:
        weights = s_ref[rows, :] * inverse
        grad = (weights * (p_ref[rows, :] - delta)).astype(BF16)
        acc_ref[rows, :] += dot(weights.astype(BF16), g_only, 1, 0) + dot(grad, q_only, 1, 0)
        part = dot(kt_ref[:, rows], grad, 1, 0)
        dq = part if dq is None else dq + part
    dq = (dq * factor).T
    dq_ref[...] = jnp.concatenate([dq[: tgt // 2], dq[tgt // 2 :]], axis=1).astype(BF16)

    @pl.when(step == pl.num_programs(1) - 1)
    def _():
        acc = acc_ref[...]
        in_key = lax.broadcasted_iota(jnp.int32, acc.shape, 1) < HD
        dkv_ref[...] = jnp.where(in_key, acc * factor, acc).astype(BF16)


def attention(qg, kv, block, chunk):
    heads, tgt, wide = qg.shape
    src = kv.shape[1]
    kt = kv[:, :, :HD].transpose(0, 2, 1)
    flops = 5 * 2 * heads * tgt * src * HD
    return pl.pallas_call(
        functools.partial(attention_kernel, chunk),
        grid=(heads, tgt // block),
        in_specs=[
            pl.BlockSpec((None, block, wide), lambda h, i: (h, i, 0)),
            pl.BlockSpec((None, src, wide), lambda h, i: (h, 0, 0)),
            pl.BlockSpec((None, HD, src), lambda h, i: (h, 0, 0)),
        ],
        out_specs=[
            pl.BlockSpec((None, block // 2, wide), lambda h, i: (h, i, 0)),
            pl.BlockSpec((None, src, wide), lambda h, i: (h, 0, 0)),
        ],
        out_shape=[
            jax.ShapeDtypeStruct((heads, tgt // 2, wide), BF16),
            jax.ShapeDtypeStruct((heads, src, wide), BF16),
        ],
        scratch_shapes=[
            pltpu.VMEM((src, block), F32),
            pltpu.VMEM((src, block), F32),
            pltpu.VMEM((src, wide), F32),
        ],
        compiler_params=pltpu.CompilerParams(vmem_limit_bytes=50 * 1024 * 1024),
        cost_estimate=pl.CostEstimate(
            flops=4 * flops, bytes_accessed=4 * heads * (tgt + src) * wide, transcendentals=heads * tgt * src
        ),
    )(qg, kv, kt)


def local(seq, col, memory, query, out_grad, w_key, w_value):
    tgt, width = query.shape
    heads = width // HD
    groups = math.gcd(heads, seq)
    ranges = seq // groups
    each = heads // groups
    same_range = [[r * groups + g for g in range(groups)] for r in range(ranges)]
    same_heads = [[r * groups + g for r in range(ranges)] for g in range(groups)]

    def deal(x):
        return lax.all_to_all(x, "seq", 0, 0, tiled=True, axis_index_groups=same_range)

    def shift(x, by):
        return lax.ppermute(x, "col", [(i, (i + by) % col) for i in range(col)])

    def pair(a, b):
        rows = a.shape[0]
        a, b = a.reshape(rows, heads, HD), b.reshape(rows, heads, HD)
        return jnp.concatenate([a, b], axis=-1).transpose(1, 0, 2)

    own = lax.all_to_all(memory, "seq", split_axis=0, concat_axis=1, tiled=True)
    rows = own.shape[0]
    mem = [own] + [shift(own, by) for by in range(1, col)]

    qg = deal(pair(query, out_grad))
    qg = qg.reshape(groups, each, tgt, 2 * HD).transpose(1, 0, 2, 3).reshape(each, groups * tgt, 2 * HD)

    mem = jnp.concatenate(mem, axis=0)
    total = mem.shape[0]
    kv = pair(dot(mem, w_key, 1, 0).astype(BF16), dot(mem, w_value, 1, 0).astype(BF16))
    kv = deal(kv)
    if ranges > 1:
        kv = lax.all_gather(kv, "seq", axis=0, tiled=True, axis_index_groups=same_heads)
    kv = kv.reshape(seq, each, total, 2 * HD).transpose(1, 0, 2, 3).reshape(each, seq * total, 2 * HD)

    dq, dkv = attention(qg, kv, tgt, 256)

    dq = dq.reshape(each, groups, tgt // 2, 2 * HD).transpose(1, 0, 2, 3)
    dq = deal(dq.reshape(heads, tgt // 2, 2 * HD))
    dq = dq.reshape(heads, tgt // 2, 2, HD).transpose(2, 1, 0, 3).reshape(tgt, width)

    dkv = dkv.reshape(each, seq, total, 2 * HD).transpose(1, 0, 2, 3).reshape(seq * each, total, 2 * HD)
    if ranges > 1:
        dkv = lax.psum_scatter(dkv, "seq", scatter_dimension=0, tiled=True, axis_index_groups=same_heads)
    dkv = deal(dkv).reshape(heads, total, 2, HD).transpose(2, 1, 0, 3).reshape(2, total, width)

    part = dot(dkv[0], w_key, 1, 1) + dot(dkv[1], w_value, 1, 1)
    summed = part[:rows]
    for by in range(1, col):
        summed = summed + shift(part[by * rows : (by + 1) * rows].astype(BF16), col - by).astype(F32)
    d_memory = lax.all_to_all(summed.astype(BF16), "seq", split_axis=1, concat_axis=0, tiled=True)
    return dq, d_memory


def solution(mesh):
    return jax.shard_map(
        functools.partial(local, mesh.shape["seq"], mesh.shape["col"]),
        mesh=mesh,
        in_specs=(
            P("col", "seq"),
            P("seq", "col"),
            P("seq", "col"),
            P(None, "col"),
            P(None, "col"),
        ),
        out_specs=(P("seq", "col"), P("col", "seq")),
        check_vma=False,
    )
```

time: 415 us -> 182 us (0.44)
  waiting for transfers between devices: 223 us -> 62.8 us
  matrix products: 101 us -> 21.9 us
  Pallas kernels: 0 us -> 35.9 us
  starting transfers between devices: 5.86 us -> 28.7 us
  local copies, waits for them, and re-layouts: 30.9 us -> 9.78 us
  other arithmetic: 17.7 us -> 3.01 us
  between operations: 14.2 us -> 0.81 us
    unnamed x8 -> x0, waiting for transfers between devices: 124 us -> none
    all_gather x3 -> x0, waiting for transfers between devices: 75 us -> none  [the longest x1 44.7 us: local(): lax.all_gather(key_local, 'seq', axis=0, tiled=True)]
    dot_general x9 -> x4, matrix products: 82.4 us -> 21.9 us  [dot(): lax.dot_general(a, b, (((over_a,), (over_b,)), ((), ())), preferred_eleme...]
    all_to_all x1 -> x5, waiting for transfers between devices: 3.59 us -> 47.3 us  [the longest x3 23.2 us: deal(): lax.all_to_all(x, 'seq', 0, 0, tiled=True, axis_index_groups=same_range)]
    pallas_call x0 -> x1, Pallas kernels: none -> 35.9 us  [attention(): pl.pallas_call(functools.partial(attention_kernel, chunk), grid=(heads, t...]
    all_to_all x1 -> x5, starting transfers between devices: 5.62 us -> 26.6 us  [the longest x3 15.1 us: deal(): lax.all_to_all(x, 'seq', 0, 0, tiled=True, axis_index_groups=same_range)]
    reduce_scatter x1 -> x0, waiting for transfers between devices: 19.6 us -> none  [local(): lax.psum_scatter(partial_value.astype(jnp.bfloat16), 'col', scatter_dimen...]
    sub x1 -> x0, matrix products: 18.1 us -> none  [local(): expo = jnp.exp(scores - row_max)]
  transfers between devices with their start and end apart: 7 -> 7, of which waited for: 7 -> 7; matrix products, arithmetic and copies ran while one was open for 20% -> 11% of each run, Pallas kernels for 0% -> 0%
where the time goes in v1:
time: 182 us; the launch traced here: 181 us
  waiting for transfers between devices  62.8 us (35%)
  Pallas kernels  35.9 us (20%)
  starting transfers between devices  28.7 us (16%)
  matrix products  21.9 us (12%)
  blocking collectives  18.4 us (10%)
  local copies, waits for them, and re-layouts  9.78 us (5%)
  other arithmetic  3.01 us (2%)
    pallas_call x1, Pallas kernels, attention(): pl.pallas_call(functools.partial(attention_kernel, chunk), grid=(heads, t...  35.9 us
    all_to_all x3, waiting for transfers between devices, deal(): lax.all_to_all(x, 'seq', 0, 0, tiled=True, axis_index_groups=same_range)  23.2 us
    dot_general x4, matrix products, dot(): lax.dot_general(a, b, (((over_a,), (over_b,)), ((), ())), preferred_eleme...  21.9 us
    all_to_all x1, blocking collectives, deal(): lax.all_to_all(x, 'seq', 0, 0, tiled=True, axis_index_groups=same_range)  18.4 us
    ppermute x2, waiting for transfers between devices, shift(): return lax.ppermute(x, 'col', [(i, (i + by) % col) for i in range(col)])  15.5 us
    all_to_all x3, starting transfers between devices, deal(): lax.all_to_all(x, 'seq', 0, 0, tiled=True, axis_index_groups=same_range)  15.1 us
    all_to_all x1, waiting for transfers between devices, local(): lax.all_to_all(summed.astype(BF16), 'seq', split_axis=1, concat_axis=0, t...  12.2 us
    all_to_all x1, waiting for transfers between devices, local(): own = lax.all_to_all(memory, 'seq', split_axis=0, concat_axis=1, tiled=True)  12 us
  transfers between devices with their start and end apart: 7, of which 7 were waited for; matrix products, arithmetic and copies ran while one was open for 11% of the time, Pallas kernels for 0%

profile of v1, /device:TPU:0, one launch (start us, length us, event | category | flops | bytes accessed | tf_op | source)
XLA Modules:
  0.0 181.2 jit_solution(4445107337746634268)
XLA Ops:
  0.6 7.4 %all-to-all-start.1 = ((bf16[16,64,256]{2,1,0:T(8,128)(2,1)}), bf16[16,64,256]{2,1,0:T(8,128)(2,1)S(1)}, u32[]{:S(2)}, u32[]{:S(2)}) async-start(bf16[16,64,256]{2,1,0:T(8,128)(2,1)} %bitcast.60), calls=%async_computation.1 | async-start | bytes 1048576 | tf_op jit(solution)/shard_map/all_to_all | solution.py:132
  8.0 1.2 copy.27
  9.3 1.2 copy.28
  10.5 12.0 %all-to-all-done.1 = bf16[16,64,256]{2,1,0:T(8,128)(2,1)S(1)} async-done(((bf16[16,64,256]{2,1,0:T(8,128)(2,1)}), bf16[16,64,256]{2,1,0:T(8,128)(2,1)S(1)}, u32[]{:S(2)}, u32[]{:S(2)}) %all-to-all-start.1) | async-done | bytes 524320 | tf_op jit(solution)/shard_map/all_to_all | solution.py:132
  22.5 1.6 collective-permute-start
  24.1 1.0 maximum_bitcast_fusion
  25.1 4.1 %all-to-all-start = ((bf16[16,256,128]{1,2,0:T(8,128)(2,1)}), bf16[16,256,128]{1,2,0:T(8,128)(2,1)S(1)}, u32[]{:S(2)}, u32[]{:S(2)}) async-start(bf16[16,256,128]{1,2,0:T(8,128)(2,1)} %maximum_bitcast_fusion), calls=%async_computation | async-start | bytes 2097152 | tf_op jit(solution)/shard_map/all_to_all | solution.py:122
  29.3 7.2 %collective-permute-done = bf16[64,4096]{1,0:T(8,128)(2,1)S(1)} collective-permute-done((bf16[64,4096]{1,0:T(8,128)(2,1)S(1)}, bf16[64,4096]{1,0:T(8,128)(2,1)S(1)}, u32[]{:S(2)}, u32[]{:S(2)}) %collective-permute-start) | collective-permute-done | bytes 524320 | tf_op jit(solution)/shard_map/ppermute | solution.py:125
  36.5 4.6 %convolution_convert_fusion.1 = bf16[128,1024]{1,0:T(8,128)(2,1)S(1)} fusion(bf16[128,4096]{1,0:T(8,128)(2,1)S(1)} %constant_dynamic-update-slice_fusion, bf16[4096,1024]{1,0:T(8,128)(2,1)} %param.8), kind=kOutput, calls=%fused_computation.2 | convolution fusion | flops 1073872896 | bytes 9699328 | tf_op jit(solution)/shard_map/dot_general | solution.py:17
  41.3 4.6 %convolution_convert_fusion = bf16[128,1024]{1,0:T(8,128)(2,1)S(1)} fusion(bf16[128,4096]{1,0:T(8,128)(2,1)S(1)} %constant_dynamic-update-slice_fusion, bf16[4096,1024]{1,0:T(8,128)(2,1)} %param.9), kind=kOutput, calls=%fused_computation.1 | convolution fusion | flops 1073872896 | bytes 9699328 | tf_op jit(solution)/shard_map/dot_general | solution.py:17
  47.0 5.2 %all-to-all-done = bf16[16,256,128]{1,2,0:T(8,128)(2,1)S(1)} async-done(((bf16[16,256,128]{1,2,0:T(8,128)(2,1)}), bf16[16,256,128]{1,2,0:T(8,128)(2,1)S(1)}, u32[]{:S(2)}, u32[]{:S(2)}) %all-to-all-start) | async-done | bytes 1048608 | tf_op jit(solution)/shard_map/all_to_all | solution.py:122
  52.2 6.9 %all-to-all-start.2 = ((bf16[16,128,128]{1,2,0:T(8,128)(2,1)}), bf16[16,128,128]{1,2,0:T(8,128)(2,1)S(1)}, u32[]{:S(2)}, u32[]{:S(2)}) async-start(bf16[16,128,128]{1,2,0:T(8,128)(2,1)} %maximum_bitcast_fusion.1), calls=%async_computation.2 | async-start | bytes 1048576 | tf_op jit(solution)/shard_map/all_to_all | solution.py:122
  59.7 13.8 %all-to-all-done.2 = bf16[16,128,128]{1,2,0:T(8,128)(2,1)S(1)} async-done(((bf16[16,128,128]{1,2,0:T(8,128)(2,1)}), bf16[16,128,128]{1,2,0:T(8,128)(2,1)S(1)}, u32[]{:S(2)}, u32[]{:S(2)}) %all-to-all-start.2) | async-done | bytes 524320 | tf_op jit(solution)/shard_map/all_to_all | solution.py:122
  74.4 35.9 %shard_map.68 = (bf16[1,2048,128]{2,1,0:T(8,128)(2,1)S(1)}, bf16[1,2048,128]{2,1,0:T(8,128)(2,1)S(1)}) custom-call(bf16[1,4096,128]{2,1,0:T(8,128)(2,1)S(1)} %bitcast.44, bf16[1,2048,128]{2,1,0:T(8,128)(2,1)S(1)} %copy.34.kv_ref, bf16[1,64,2048]{2,1,0:T(8,128)(2,1)S(1)} %slice_bitcast_fusion.kt_ref), custom_call_target="tpu_custom_call" | custom-call | flops 21474836480 | bytes 3145728 | tf_op jit(solution)/shard_map/pallas_call | solution.py:84
  110.6 18.4 %all_to_all.58 = bf16[16,128,128]{1,2,0:T(8,128)(2,1)S(1)} all-to-all(bf16[16,128,128]{1,2,0:T(8,128)(2,1)S(1)} %copy.37), channel_id=1, replica_groups={{0,2,4,6,8,10,12,14,16,18,20,22,24,26,28,30},{1,3,5,7,9,11,13,15,17,19,..., dimensions={0} | all-to-all | bytes 1048576 | tf_op jit(solution)/shard_map/all_to_all | solution.py:122
  129.0 6.3 %fusion.2 = f32[128,4096]{1,0:T(8,128)S(1)} fusion(bf16[128,1024]{0,1:T(8,128)(2,1)S(1)} %bitcast.59, bf16[4096,1024]{1,0:T(8,128)(2,1)} %param.8), kind=kOutput, calls=%fused_computation.13 | convolution fusion | flops 1073741824 | bytes 10747904 | tf_op jit(solution)/shard_map/dot_general | solution.py:17
  135.3 6.3 %convolution_add_fusion = f32[128,4096]{1,0:T(8,128)S(1)} fusion(f32[128,4096]{1,0:T(8,128)S(1)} %fusion.2, bf16[128,1024]{0,1:T(8,128)(2,1)S(1)} %bitcast.56, bf16[4096,1024]{1,0:T(8,128)(2,1)} %param.9), kind=kOutput, calls=%fused_computation | convolution fusion | flops 1074266112 | bytes 12845056 | tf_op jit(solution)/shard_map/dot_general | solution.py:17
  143.3 4.1 %all-to-all-start.3 = ((bf16[16,128,128]{1,2,0:T(8,128)(2,1)}), bf16[16,128,128]{1,2,0:T(8,128)(2,1)S(1)}, u32[]{:S(2)}, u32[]{:S(2)}) async-start(bf16[16,128,128]{1,2,0:T(8,128)(2,1)} %copy.35), calls=%async_computation.3 | async-start | bytes 1048576 | tf_op jit(solution)/shard_map/all_to_all | solution.py:122
  147.4 8.3 %collective-permute-done.1 = bf16[64,4096]{1,0:T(8,128)(2,1)} collective-permute-done((bf16[64,4096]{1,0:T(8,128)(2,1)S(1)}, bf16[64,4096]{1,0:T(8,128)(2,1)}, u32[]{:S(2)}, u32[]{:S(2)}) %collective-permute-start.1) | collective-permute-done | bytes 524320 | tf_op jit(solution)/shard_map/ppermute | solution.py:125
  155.7 1.1 fusion
  157.7 4.2 %all-to-all-done.3 = bf16[16,128,128]{1,2,0:T(8,128)(2,1)S(1)} async-done(((bf16[16,128,128]{1,2,0:T(8,128)(2,1)}), bf16[16,128,128]{1,2,0:T(8,128)(2,1)S(1)}, u32[]{:S(2)}, u32[]{:S(2)}) %all-to-all-start.3) | async-done | bytes 524320 | tf_op jit(solution)/shard_map/all_to_all | solution.py:122
  161.9 4.1 %all-to-all-start.5 = ((bf16[64,16,256]{2,0,1:T(8,128)(2,1)}), bf16[64,16,256]{2,0,1:T(8,128)(2,1)S(1)}, u32[]{:S(2)}, u32[]{:S(2)}) async-start(bf16[64,16,256]{2,0,1:T(8,128)(2,1)} %bitcast.43), calls=%async_computation.5 | async-start | bytes 1048576 | tf_op jit(solution)/shard_map/all_to_all | solution.py:162
  166.8 1.5 reshape.43
  168.3 12.2 %all-to-all-done.5 = bf16[64,16,256]{2,0,1:T(8,128)(2,1)S(1)} async-done(((bf16[64,16,256]{2,0,1:T(8,128)(2,1)}), bf16[64,16,256]{2,0,1:T(8,128)(2,1)S(1)}, u32[]{:S(2)}, u32[]{:S(2)}) %all-to-all-start.5) | async-done | bytes 524320 | tf_op jit(solution)/shard_map/all_to_all | solution.py:162
  (19 shorter events, 7.2 us)
Async XLA Ops:
  0.6 21.9 %all-to-all-start.1 = ((bf16[16,64,256]{2,1,0:T(8,128)(2,1)}), bf16[16,64,256]{2,1,0:T(8,128)(2,1)S(1)}, u32[]{:S(2)}, u32[]{:S(2)}) async-start(bf16[16,64,256]{2,1,0:T(8,128)(2,1)} %bitcast.60), calls=%async_computation.1 | async-start | bytes 1048576 | tf_op jit(solution)/shard_map/all_to_all | solution.py:132
  22.5 13.9 %collective-permute-start = (bf16[64,4096]{1,0:T(8,128)(2,1)S(1)}, bf16[64,4096]{1,0:T(8,128)(2,1)S(1)}, u32[]{:S(2)}, u32[]{:S(2)}) collective-permute-start(bf16[64,4096]{1,0:T(8,128)(2,1)S(1)} %bitcast.48), channel_id=1, source_target_pairs={{0,1},{1,0},{2,3},{3,2},{4,5},{5,4},{6,7},{7,6},{8,9},{9,8},{10,11... | collective-permute-start | bytes 1572872 | tf_op jit(solution)/shard_map/ppermute | solution.py:125
  25.1 27.0 %all-to-all-start = ((bf16[16,256,128]{1,2,0:T(8,128)(2,1)}), bf16[16,256,128]{1,2,0:T(8,128)(2,1)S(1)}, u32[]{:S(2)}, u32[]{:S(2)}) async-start(bf16[16,256,128]{1,2,0:T(8,128)(2,1)} %maximum_bitcast_fusion), calls=%async_computation | async-start | bytes 2097152 | tf_op jit(solution)/shard_map/all_to_all | solution.py:122
  52.2 21.3 %all-to-all-start.2 = ((bf16[16,128,128]{1,2,0:T(8,128)(2,1)}), bf16[16,128,128]{1,2,0:T(8,128)(2,1)S(1)}, u32[]{:S(2)}, u32[]{:S(2)}) async-start(bf16[16,128,128]{1,2,0:T(8,128)(2,1)} %maximum_bitcast_fusion.1), calls=%async_computation.2 | async-start | bytes 1048576 | tf_op jit(solution)/shard_map/all_to_all | solution.py:122
  141.7 14.0 %collective-permute-start.1 = (bf16[64,4096]{1,0:T(8,128)(2,1)S(1)}, bf16[64,4096]{1,0:T(8,128)(2,1)}, u32[]{:S(2)}, u32[]{:S(2)}) collective-permute-start(bf16[64,4096]{1,0:T(8,128)(2,1)S(1)} %slice.33), channel_id=1, source_target_pairs={{0,1},{1,0},{2,3},{3,2},{4,5},{5,4},{6,7},{7,6},{8,9},{9,8},{10,11... | collective-permute-start | bytes 1572872 | tf_op jit(solution)/shard_map/ppermute | solution.py:125
  143.3 18.6 %all-to-all-start.3 = ((bf16[16,128,128]{1,2,0:T(8,128)(2,1)}), bf16[16,128,128]{1,2,0:T(8,128)(2,1)S(1)}, u32[]{:S(2)}, u32[]{:S(2)}) async-start(bf16[16,128,128]{1,2,0:T(8,128)(2,1)} %copy.35), calls=%async_computation.3 | async-start | bytes 1048576 | tf_op jit(solution)/shard_map/all_to_all | solution.py:122
  161.9 18.6 %all-to-all-start.5 = ((bf16[64,16,256]{2,0,1:T(8,128)(2,1)}), bf16[64,16,256]{2,0,1:T(8,128)(2,1)S(1)}, u32[]{:S(2)}, u32[]{:S(2)}) async-start(bf16[64,16,256]{2,0,1:T(8,128)(2,1)} %bitcast.43), calls=%async_computation.5 | async-start | bytes 1048576 | tf_op jit(solution)/shard_map/all_to_all | solution.py:162

commit v2 on v1

v2 whole, which is shorter than its diff:
```python
import functools
import math

import jax
import jax.numpy as jnp
from jax import lax
from jax.experimental import pallas as pl
from jax.experimental.pallas import tpu as pltpu
from jax.sharding import PartitionSpec as P

HD = 64
F32 = jnp.float32
BF16 = jnp.bfloat16
VMEM = pl.BlockSpec(memory_space=pltpu.VMEM)
SMEM = pl.BlockSpec(memory_space=pltpu.SMEM)
MIB = 1024 * 1024


def dot(a, b, over_a, over_b):
    return lax.dot_general(
        a, b, (((over_a,), (over_b,)), ((), ())), preferred_element_type=F32
    )


def whole(kernel, out, *args, after=(), scratch=(), limit=24, flops=0):
    n = len(args)
    moved = sum(x.size * x.dtype.itemsize for x in args)
    return pl.pallas_call(
        lambda *refs: kernel(*refs[:n], *refs[n + len(after) :]),
        in_specs=[SMEM if x.dtype == jnp.int32 else VMEM for x in args]
        + [pl.BlockSpec(memory_space=pl.ANY)] * len(after),
        out_specs=[VMEM] * len(out),
        out_shape=out,
        scratch_shapes=scratch,
        compiler_params=pltpu.CompilerParams(vmem_limit_bytes=limit * MIB),
        cost_estimate=pl.CostEstimate(flops=flops, bytes_accessed=moved, transcendentals=0),
    )(*args, *after)


def head_of(x, h):
    return x[:, h * HD : (h + 1) * HD]


def pair_heads(query, out_grad):
    tgt, width = query.shape

    def kernel(q_ref, g_ref, out_ref):
        for h in range(width // HD):
            cols = pl.ds(h * HD, HD)
            out_ref[h] = jnp.concatenate([q_ref[:, cols], g_ref[:, cols]], axis=1)

    out = [jax.ShapeDtypeStruct((width // HD, tgt, 2 * HD), BF16)]
    return whole(kernel, out, query, out_grad)[0]


def pair_targets(query, out_grad, me, spans):
    tgt, width = query.shape
    place = [(i, at) for i, span in enumerate(spans) for at in range(len(span))]
    out = [
        jax.ShapeDtypeStruct((len(span), 2, tgt, 2 * HD), BF16) for span in spans for _ in range(2)
    ]

    def kernel(me_ref, q_ref, g_ref, *rest):
        out_refs, paired = rest[:-1], rest[-1]
        for h in range(width // HD):
            cols = pl.ds(h * HD, HD)
            paired[h] = jnp.concatenate([q_ref[:, cols], g_ref[:, cols]], axis=1)
        for i, at in place:
            for bits in range(4):
                head = (4 * spans[i][at] + bits) ^ me_ref[0]
                out_refs[2 * i + bits // 2][at, bits % 2] = paired[head]

    scratch = [pltpu.VMEM((width // HD, tgt, 2 * HD), BF16)]
    return whole(kernel, out, me, query, out_grad, scratch=scratch)


def cross(kept, came, after=()):
    def kernel(kept_ref, came_ref, first_ref, second_ref):
        for i, ref in enumerate((kept_ref, came_ref)):
            first_ref[:, i] = ref[:, 0]
            second_ref[:, i] = ref[:, 1]

    out = [jax.ShapeDtypeStruct(kept.shape, kept.dtype)] * 2
    return whole(kernel, out, kept, came, after=after)


def join(kept, came, after=()):
    def kernel(kept_ref, came_ref, *out_refs):
        for d, out_ref in enumerate(out_refs):
            out_ref[0] = kept_ref[d]
            out_ref[1] = came_ref[d]

    out = [jax.ShapeDtypeStruct((2, *kept.shape[1:]), kept.dtype)] * kept.shape[0]
    return whole(kernel, out, kept, came, after=after)


def part_ways(pieces, after=()):
    def kernel(*refs):
        kept_ref, left_ref = refs[-2:]
        for d, ref in enumerate(refs[:-2]):
            kept_ref[d] = ref[0]
            left_ref[d] = ref[1]

    out = [jax.ShapeDtypeStruct((len(pieces), *pieces[0].shape[1:]), pieces[0].dtype)] * 2
    return whole(kernel, out, *pieces, after=after)


def concat(pieces, after=()):
    rows = [x.shape[0] for x in pieces]

    def kernel(*refs):
        at = 0
        for ref, n in zip(refs[:-1], rows):
            refs[-1][at : at + n] = ref[...]
            at += n

    out = [jax.ShapeDtypeStruct((sum(rows), *pieces[0].shape[1:]), pieces[0].dtype)]
    return whole(kernel, out, *pieces, after=after)[0]


def project(mem, w_key, w_value, before=None, after=()):
    blocks, rows, depth = mem.shape
    depth *= blocks
    width = w_key.shape[1]
    heads = width // HD
    tile = math.gcd(width, 256)
    ahead = 0 if before is None else before.shape[1]

    def kernel(m_ref, k_ref, v_ref, *refs):
        out_ref = refs[-1]
        if ahead:
            out_ref[:, :ahead, :] = refs[0][...]
        m = jnp.concatenate([m_ref[b] for b in range(blocks)], axis=1)
        for at in range(0, width, tile):
            key = dot(m, k_ref[:, at : at + tile], 1, 0).astype(BF16)
            value = dot(m, v_ref[:, at : at + tile], 1, 0).astype(BF16)
            for h in range(tile // HD):
                out_ref[at // HD + h, ahead:, :] = jnp.concatenate(
                    [head_of(key, h), head_of(value, h)], axis=1
                )

    out = [jax.ShapeDtypeStruct((heads, ahead + rows, 2 * HD), BF16)]
    args = (mem, w_key, w_value) + (() if before is None else (before,))
    return whole(kernel, out, *args, after=after, flops=4 * rows * depth * width)[0]


def memory_grad(dkv, at, rows, w_key, w_value, blocks, dtype, span=(0, 1), after=()):
    heads = dkv.shape[0]
    depth, width = w_key.shape
    each = depth // blocks
    tile = max(each, math.gcd(depth, 512))
    low, high = (int(depth * x) // tile * tile for x in span)

    def kernel(d_ref, k_ref, v_ref, out_ref):
        d = [d_ref[h, at : at + rows, :] for h in range(heads)]
        dk = jnp.concatenate([x[:, :HD] for x in d], axis=1)
        dv = jnp.concatenate([x[:, HD:] for x in d], axis=1)
        for start in range(low, high, tile):
            here = pl.ds(start, tile)
            part = dot(k_ref[here, :], dk, 1, 1) + dot(v_ref[here, :], dv, 1, 1)
            part = part.T.astype(dtype)
            for b in range(tile // each):
                out_ref[(start - low) // each + b] = part[:, b * each : (b + 1) * each]

    out = [jax.ShapeDtypeStruct(((high - low) // each, rows, each), dtype)]
    flops = 4 * rows * (high - low) * width
    return whole(kernel, out, dkv, w_key, w_value, after=after, flops=flops)[0]


def add_up(parts, others, after=()):
    def kernel(*refs):
        out_ref, at = refs[-1], 0
        for ref in refs[: len(parts)]:
            here = pl.ds(at, ref.shape[0])
            total = ref[...]
            for other in refs[len(parts) : -1]:
                total = total + other[here].astype(F32)
            out_ref[here] = total.astype(BF16)
            at += ref.shape[0]

    out = [jax.ShapeDtypeStruct((sum(x.shape[0] for x in parts), *parts[0].shape[1:]), BF16)]
    return whole(kernel, out, *parts, *others, after=after)[0]


def unpack_query_grad(kept, came, me):
    far, _, half, wide = kept.shape
    heads = 4 * far

    def kernel(me_ref, kept_ref, came_ref, out_ref, by_head):
        for d in range(far):
            for bits in range(4):
                ref = came_ref if bits // 2 else kept_ref
                by_head[(4 * d + bits) ^ me_ref[0]] = ref[d, bits % 2]
        for side in range(2):
            rows = [by_head[h][:, side * HD : (side + 1) * HD] for h in range(heads)]
            out_ref[pl.ds(side * half, half), :] = jnp.concatenate(rows, axis=1)

    out = [jax.ShapeDtypeStruct((2 * half, heads * HD), BF16)]
    return whole(kernel, out, me, kept, came, scratch=[pltpu.VMEM((heads, half, wide), BF16)])[0]


def fold_rows(x, combine):
    return combine(x.reshape(x.shape[0] // 8, 8, x.shape[1]), axis=0)


def attention_kernel(chunk, rows, first, last, qg_ref, kv_ref, *refs):
    step = pl.program_id(1)
    begin = (pl.program_id(0) == 0) & (step == 0)
    end = (pl.program_id(0) == pl.num_programs(0) - 1) & (step == pl.num_programs(1) - 1)
    if not first:
        before_ref, *refs = refs
    if last:
        wk_ref, wv_ref, dq_ref, dkv_ref, wk_out, wv_out, sem, *refs = refs
    else:
        dq_ref, dkv_ref, *refs = refs
    s_ref, p_ref, acc_ref, kt_ref = refs

    fetches = []
    if last:
        fetches.append(pltpu.make_async_copy(wk_ref, wk_out, sem.at[0]))
        fetches.append(pltpu.make_async_copy(wv_ref, wv_out, sem.at[1]))

    @pl.when(begin)
    def _():
        for fetch in fetches:
            fetch.start()

    src, tgt = kv_ref.shape[0], qg_ref.shape[0]
    factor = 1.0 / math.sqrt(HD)
    slope = factor * math.log2(math.e)

    @pl.when(step == 0)
    def _():
        acc_ref[...] = jnp.zeros_like(acc_ref) if first else before_ref[...]
        kt_ref[...] = kv_ref[...].T[:HD]

    qg = qg_ref[...]
    in_query = lax.broadcasted_iota(jnp.int32, qg.shape, 1) < HD
    zero = jnp.zeros_like(qg)
    q_only = jnp.where(in_query, qg, zero)
    g_only = jnp.where(in_query, zero, qg)

    chunks = [pl.ds(at, chunk) for at in range(0, src, chunk)]
    top = None
    for here in chunks:
        s = dot(kv_ref[here, :], q_only, 1, 1)
        s_ref[here, :] = s
        s = fold_rows(s, jnp.max)
        top = s if top is None else jnp.maximum(top, s)
    top = jnp.max(top, axis=0, keepdims=True)

    total = inner = None
    for here in chunks:
        expo = jnp.exp2((s_ref[here, :] - top) * slope)
        p = dot(kv_ref[here, :], g_only, 1, 1)
        s_ref[here, :] = expo
        p_ref[here, :] = p
        t, i = fold_rows(expo, jnp.sum), fold_rows(expo * p, jnp.sum)
        total, inner = (t, i) if total is None else (total + t, inner + i)
    inverse = 1.0 / jnp.sum(total, axis=0, keepdims=True)
    delta = jnp.sum(inner, axis=0, keepdims=True) * inverse

    dq = None
    for here in chunks:
        weights = s_ref[here, :] * inverse
        grad = (weights * (p_ref[here, :] - delta)).astype(BF16)
        acc_ref[here, :] += dot(weights.astype(BF16), g_only, 1, 0) + dot(grad, q_only, 1, 0)
        part = dot(kt_ref[:, here], grad, 1, 0)
        dq = part if dq is None else dq + part
    dq = (dq * factor).T
    half = rows // 2
    for at in range(0, tgt, rows):
        dq_ref[at // 2 : at // 2 + half, :] = jnp.concatenate(
            [dq[at : at + half], dq[at + half : at + rows]], axis=1
        ).astype(BF16)

    @pl.when(step == pl.num_programs(1) - 1)
    def _():
        acc = acc_ref[...]
        if last:
            in_key = lax.broadcasted_iota(jnp.int32, acc.shape, 1) < HD
            acc = jnp.where(in_key, acc * factor, acc)
        dkv_ref[...] = acc.astype(dkv_ref.dtype)

    @pl.when(end)
    def _():
        for fetch in fetches:
            fetch.wait()


def attention(qg, kv, rows, before=None, weights=(), block=512, chunk=256):
    heads, tgt, wide = qg.shape
    src = kv.shape[1]
    first, last = before is None, bool(weights)
    work = heads * tgt * src
    block = max(math.gcd(tgt, block), rows)
    every = pl.BlockSpec((None, src, wide), lambda h, i: (h, 0, 0))
    anywhere = pl.BlockSpec(memory_space=pl.ANY)
    return pl.pallas_call(
        functools.partial(attention_kernel, chunk, rows, first, last),
        grid=(heads, tgt // block),
        in_specs=[pl.BlockSpec((None, block, wide), lambda h, i: (h, i, 0)), every]
        + [every] * (not first)
        + [anywhere] * len(weights),
        out_specs=[pl.BlockSpec((None, block // 2, wide), lambda h, i: (h, i, 0)), every]
        + [anywhere] * len(weights),
        out_shape=[
            jax.ShapeDtypeStruct((heads, tgt // 2, wide), BF16),
            jax.ShapeDtypeStruct((heads, src, wide), BF16 if last else F32),
        ]
        + [pltpu.VMEM(w.shape, w.dtype) for w in weights],
        scratch_shapes=[pltpu.SemaphoreType.DMA((2,))] * last
        + [
            pltpu.VMEM((src, block), F32),
            pltpu.VMEM((src, block), F32),
            pltpu.VMEM((src, wide), F32),
            pltpu.VMEM((HD, src), BF16),
        ],
        compiler_params=pltpu.CompilerParams(vmem_limit_bytes=32 * MIB),
        cost_estimate=pl.CostEstimate(
            flops=5 * 8 * work * HD, bytes_accessed=8 * heads * (tgt + src) * wide, transcendentals=work
        ),
    )(qg, kv, *(() if first else (before,)), *weights)


def local(seq, col, memory, query, out_grad, w_key, w_value):
    tgt, width = query.shape
    heads = width // HD
    groups = math.gcd(heads, seq)
    ranges = seq // groups
    each = heads // groups
    same_range = [[r * groups + g for g in range(groups)] for r in range(ranges)]
    same_heads = [[r * groups + g for r in range(ranges)] for g in range(groups)]
    pairwise = ranges == 1 and each == 1 and groups >= 16 and groups & (groups - 1) == 0
    me = lax.axis_index("seq").astype(jnp.int32) if pairwise else jnp.int32(0)
    me = me.reshape(1)
    far = groups // 4

    def deal(x):
        return lax.all_to_all(x, "seq", 0, 0, tiled=True, axis_index_groups=same_range)

    def swap(x, bits):
        return lax.ppermute(x, "seq", [(i, i ^ bits) for i in range(seq)])

    def gather_far(x, d):
        return swap(x, 4 * d) if d else x

    def by_head(x, many):
        x = x.reshape(many, each, *x.shape[1:]).swapaxes(0, 1)
        return x.reshape(each, many * x.shape[2], x.shape[3])

    def by_owner(x, many):
        x = x.reshape(each, many, x.shape[1] // many, x.shape[2]).swapaxes(0, 1)
        return x.reshape(many * each, *x.shape[2:])

    def shift(x, by):
        return lax.ppermute(x, "col", [(i, (i + by) % col) for i in range(col)])

    rows = memory.shape[0] // seq
    total = rows * col
    own = lax.all_to_all(memory.reshape(seq, rows, -1), "seq", 0, 0, tiled=True)

    if pairwise:
        early = far // 2
        late = [d for d in range(far) if d != early]
        kept, left, kept_late, left_late = pair_targets(query, out_grad, me, [[early], late])
        kept, left = cross(kept, swap(left, 2))
        early_qg, own = lax.optimization_barrier((join(kept, swap(left, 1))[0], own))
        early_qg = gather_far(early_qg, early)
        left_late = concat([left_late], after=(own,))
        left_late = swap(left_late, 2)
        kv = project(own, w_key, w_value)
        kept, left = cross(kept_late, left_late, after=(kv, early_qg))
        late_qg = join(kept, swap(left, 1))
        for by in range(1, col):
            kv = project(shift(own, by), w_key, w_value, kv, after=(early_qg, late_qg[0]))
        kv = deal(kv)
        late_qg = [gather_far(x, d) for x, d in zip(late_qg, late)]
        qg = [[late_qg[0], early_qg], late_qg[1:]]
        order = [0, early, *late[1:]]
    else:
        qg = deal(pair_heads(query, out_grad))
        kv = project(own, w_key, w_value)
        for by in range(1, col):
            kv = project(shift(own, by), w_key, w_value, kv)
        kv = deal(kv)
        qg = [by_head(qg, groups)]
    if ranges > 1:
        kv = lax.all_gather(kv, "seq", axis=0, tiled=True, axis_index_groups=same_heads)
    kv = by_head(kv, seq)

    dq, dkv = [], None
    for i, x in enumerate(qg):
        if pairwise:
            x = concat([piece.reshape(-1, 2 * HD) for piece in x], after=(dkv,) * (i > 0))[None]
        weights = (w_key, w_value) if i == len(qg) - 1 else ()
        part, dkv, *weights = attention(x, kv, tgt, dkv, weights)
        dq.append(part)
    w_key, w_value = weights
    dkv = by_owner(dkv, seq)
    if ranges > 1:
        dkv = lax.psum_scatter(dkv, "seq", scatter_dimension=0, tiled=True, axis_index_groups=same_heads)
    dkv = deal(dkv)

    others = [memory_grad(dkv, by * rows, rows, w_key, w_value, seq, BF16) for by in range(1, col)]
    others = [shift(x, col - 1 - i) for i, x in enumerate(others)]
    mine = [memory_grad(dkv, 0, rows, w_key, w_value, seq, F32, (0, 0.25))]
    mine.append(memory_grad(dkv, 0, rows, w_key, w_value, seq, F32, (0.25, 1)))
    if pairwise:
        dq = concat([x.reshape(-1, 2, 2, tgt // 2, 2 * HD) for x in dq], after=mine[:1])
        dq = [gather_far(dq[order.index(d)], d) for d in range(far)]
        summed = add_up(mine, others, after=dq)
        kept, left = part_ways(dq, after=(summed,))
        kept, left = cross(kept, swap(left, 1))
        dq = unpack_query_grad(kept, swap(left, 2), me)
    else:
        summed = add_up(mine, others)
        dq = deal(by_owner(dq[0], groups))
        dq = dq.reshape(heads, tgt // 2, 2, HD).transpose(2, 1, 0, 3).reshape(tgt, width)
    d_memory = lax.all_to_all(summed, "seq", 0, 0, tiled=True)
    return dq, d_memory.reshape(memory.shape)


def solution(mesh):
    return jax.shard_map(
        functools.partial(local, mesh.shape["seq"], mesh.shape["col"]),
        mesh=mesh,
        in_specs=(
            P("col", "seq"),
            P("seq", "col"),
            P("seq", "col"),
            P(None, "col"),
            P(None, "col"),
        ),
        out_specs=(P("seq", "col"), P("col", "seq")),
        check_vma=False,
    )
```

time: 182 us -> 156 us (0.86)
  matrix products: 21.9 us -> 0 us
  waiting for transfers between devices: 62.8 us -> 41.8 us
  Pallas kernels: 35.9 us -> 51.6 us
  starting transfers between devices: 28.7 us -> 33.2 us
  other arithmetic: 3.01 us -> 0 us
    ppermute x0 -> x12, waiting for transfers between devices: none -> 28.1 us  [swap(): return lax.ppermute(x, 'seq', [(i, i ^ bits) for i in range(seq)])]
    dot_general x4 -> x0, matrix products: 21.9 us -> none  [dot(): lax.dot_general(a, b, (((over_a,), (over_b,)), ((), ())), preferred_eleme...]
    all_to_all x2, waiting for transfers between devices: 24.1 us -> 3.18 us  [the longest x1 3.03 us: local(): own = lax.all_to_all(memory.reshape(seq, rows, -1), 'seq', 0, 0, tiled=True)]
    pallas_call x1 -> x20, Pallas kernels: 35.9 us -> 51.6 us  [the longest x2 32.3 us: attention(): pl.pallas_call(functools.partial(attention_kernel, chunk, rows, first, la...]
    ppermute x2, waiting for transfers between devices: 15.5 us -> 0.01 us  [shift(): return lax.ppermute(x, 'col', [(i, (i + by) % col) for i in range(col)])]
    ppermute x0 -> x12, starting transfers between devices: none -> 15.4 us  [swap(): return lax.ppermute(x, 'seq', [(i, i ^ bits) for i in range(seq)])]
    all_to_all x3 -> x1, waiting for transfers between devices: 23.2 us -> 10.5 us  [deal(): lax.all_to_all(x, 'seq', 0, 0, tiled=True, axis_index_groups=same_range)]
    all_to_all x3 -> x1, starting transfers between devices: 15.1 us -> 3.77 us  [deal(): lax.all_to_all(x, 'seq', 0, 0, tiled=True, axis_index_groups=same_range)]
  transfers between devices with their start and end apart: 7 -> 17, of which waited for: 7 -> 11; matrix products, arithmetic and copies ran while one was open for 11% -> 0% of each run, Pallas kernels for 0% -> 17%
where the time goes in v2:
time: 156 us; the launch traced here: 155 us
  Pallas kernels  51.6 us (33%)
  waiting for transfers between devices  41.8 us (27%)
  starting transfers between devices  33.2 us (21%)
  blocking collectives  18.3 us (12%)
  local copies, waits for them, and re-layouts  9.68 us (6%)
    pallas_call x2, Pallas kernels, attention(): pl.pallas_call(functools.partial(attention_kernel, chunk, rows, first, la...  32.3 us
    ppermute x12, waiting for transfers between devices, swap(): return lax.ppermute(x, 'seq', [(i, i ^ bits) for i in range(seq)])  28.1 us
    pallas_call x18, Pallas kernels, whole(): pl.pallas_call(lambda *refs: kernel(*refs[:n], *refs[n + len(after):]), i...  19.3 us
    all_to_all x1, blocking collectives, deal(): lax.all_to_all(x, 'seq', 0, 0, tiled=True, axis_index_groups=same_range)  18.3 us
    ppermute x12, starting transfers between devices, swap(): return lax.ppermute(x, 'seq', [(i, i ^ bits) for i in range(seq)])  15.4 us
    all_to_all x1, waiting for transfers between devices, deal(): lax.all_to_all(x, 'seq', 0, 0, tiled=True, axis_index_groups=same_range)  10.5 us
    unnamed x13, local copies, waits for them, and re-layouts  9.64 us
    all_to_all x1, starting transfers between devices, local(): own = lax.all_to_all(memory.reshape(seq, rows, -1), 'seq', 0, 0, tiled=True)  7.4 us
  transfers between devices with their start and end apart: 17, of which 11 were waited for; matrix products, arithmetic and copies ran while one was open for 0% of the time, Pallas kernels for 17%

profile of v2, /device:TPU:0, one launch (start us, length us, event | category | flops | bytes accessed | tf_op | source)
XLA Modules:
  0.0 155.4 jit_solution(9337930446292231141)
XLA Ops:
  0.6 7.4 %all-to-all-start = ((bf16[16,64,256]{2,1,0:T(8,128)(2,1)}), bf16[16,64,256]{2,1,0:T(8,128)(2,1)S(1)}, u32[]{:S(2)}, u32[]{:S(2)}) async-start(bf16[16,64,256]{2,1,0:T(8,128)(2,1)} %bitcast.33), calls=%async_computation | async-start | bytes 1048576 | tf_op jit(solution)/shard_map/all_to_all | solution.py:361
  10.5 2.0 %collective-permute-start = (bf16[1,2,256,128]{3,2,1,0:T(8,128)(2,1)S(1)}, bf16[1,2,256,128]{3,2,1,0:T(8,128)(2,1)S(1)}, u32[]{:S(2)}, u32[]{:S(2)}) collective-permute-start(bf16[1,2,256,128]{3,2,1,0:T(8,128)(2,1)S(1)} %get-tuple-element.28), channel_id=1, source_target_pairs={{0,4},{2,6},{4,0},{6,2},{8,12},{10,14},{12,8},{14,10},{16,20},{18,... | collective-permute-start | bytes 393224 | tf_op jit(solution)/shard_map/ppermute | solution.py:343
  12.5 5.5 %collective-permute-done.refs_1_ = bf16[1,2,256,128]{3,2,1,0:T(8,128)(2,1)S(1)} collective-permute-done((bf16[1,2,256,128]{3,2,1,0:T(8,128)(2,1)S(1)}, bf16[1,2,256,128]{3,2,1,0:T(8,128)(2,1)S(1)}, u32[]{:S(2)}, u32[]{:S(2)}) %collective-permute-start) | collective-permute-done | bytes 131104 | tf_op jit(solution)/shard_map/ppermute | solution.py:343
  19.5 3.0 %all-to-all-done.refs_1_.refs_0_ = bf16[16,64,256]{2,1,0:T(8,128)(2,1)S(1)} async-done(((bf16[16,64,256]{2,1,0:T(8,128)(2,1)}), bf16[16,64,256]{2,1,0:T(8,128)(2,1)S(1)}, u32[]{:S(2)}, u32[]{:S(2)}) %all-to-all-start) | async-done | bytes 524320 | tf_op jit(solution)/shard_map/all_to_all | solution.py:361
  23.0 1.9 %collective-permute-start.3 = (bf16[2,2,256,128]{3,2,1,0:T(8,128)(2,1)S(1)}, bf16[2,2,256,128]{3,2,1,0:T(8,128)(2,1)S(1)}, u32[]{:S(2)}, u32[]{:S(2)}) collective-permute-start(bf16[2,2,256,128]{3,2,1,0:T(8,128)(2,1)S(1)} %shard_map.70), channel_id=1, source_target_pairs={{0,16},{2,18},{4,20},{6,22},{8,24},{10,26},{12,28},{14,30},{16,0},... | collective-permute-start | bytes 786440 | tf_op jit(solution)/shard_map/ppermute | solution.py:343
  26.4 3.4 %copy-done = bf16[4096,1024]{1,0:T(8,128)(2,1)S(1)} copy-done((bf16[4096,1024]{1,0:T(8,128)(2,1)S(1)}, bf16[4096,1024]{1,0:T(8,128)(2,1)}, u32[]{:S(2)}) %copy-start) | copy-done | bytes 8388632
  29.8 3.4 %copy-done.2 = bf16[4096,1024]{1,0:T(8,128)(2,1)S(1)} copy-done((bf16[4096,1024]{1,0:T(8,128)(2,1)S(1)}, bf16[4096,1024]{1,0:T(8,128)(2,1)}, u32[]{:S(2)}) %copy-start.2) | copy-done | bytes 8388632
  33.2 3.2 %shard_map.72.refs_2_.refs_3_ = bf16[16,64,128]{2,1,0:T(8,128)(2,1)S(1)} custom-call(bf16[16,64,256]{2,1,0:T(8,128)(2,1)S(1)} %all-to-all-done.refs_1_.refs_0_, bf16[4096,1024]{1,0:T(8,128)(2,1)S(1)} %copy-done, bf16[4096,1024]{1,0:T(8,128)(2,1)S(1)} %copy-done.2), custom_call_target="tpu_custom_call" | custom-call | flops 1073741824 | bytes 17301504 | tf_op jit(solution)/shard_map/pallas_call | solution.py:28
  36.4 1.8 %collective-permute-done.3.refs_3_.refs_4_ = bf16[2,2,256,128]{3,2,1,0:T(8,128)(2,1)S(1)} collective-permute-done((bf16[2,2,256,128]{3,2,1,0:T(8,128)(2,1)S(1)}, bf16[2,2,256,128]{3,2,1,0:T(8,128)(2,1)S(1)}, u32[]{:S(2)}, u32[]{:S(2)}) %collective-permute-start.3) | collective-permute-done | bytes 262176 | tf_op jit(solution)/shard_map/ppermute | solution.py:343
  40.1 3.9 %shard_map.76 = bf16[16,128,128]{2,1,0:T(8,128)(2,1)} custom-call(bf16[16,64,256]{2,1,0:T(8,128)(2,1)S(1)} %collective-permute-done.5.refs_0_, bf16[4096,1024]{1,0:T(8,128)(2,1)S(1)} %copy-done.1, bf16[4096,1024]{1,0:T(8,128)(2,1)S(1)} %copy-done.3, bf16[16,64,128]{2,1,0:T(8,128)(2,1)S(1)} %shard_map.72.refs_2_.refs_3_, ...), custom_call_target="tpu_custom_call" | custom-call | flops 1073741824 | bytes 17563648 | tf_op jit(solution)/shard_map/pallas_call | solution.py:28
  44.1 3.8 %all-to-all-start.1 = ((bf16[16,128,128]{2,1,0:T(8,128)(2,1)}), bf16[16,128,128]{2,1,0:T(8,128)(2,1)S(1)}, u32[]{:S(2)}, u32[]{:S(2)}) async-start(bf16[16,128,128]{2,1,0:T(8,128)(2,1)} %shard_map.76), calls=%async_computation.1 | async-start | bytes 1048576 | tf_op jit(solution)/shard_map/all_to_all | solution.py:340
  47.9 1.8 %collective-permute-start.6 = (bf16[2,2,256,128]{3,2,1,0:T(8,128)(2,1)S(1)}, bf16[2,2,256,128]{3,2,1,0:T(8,128)(2,1)S(1)}, u32[]{:S(2)}, u32[]{:S(2)}) collective-permute-start(bf16[2,2,256,128]{3,2,1,0:T(8,128)(2,1)S(1)} %get-tuple-element.37), channel_id=1, source_target_pairs={{0,8},{2,10},{4,12},{6,14},{8,0},{10,2},{12,4},{14,6},{16,24},{18,... | collective-permute-start | bytes 786440 | tf_op jit(solution)/shard_map/ppermute | solution.py:343
  49.7 2.4 %collective-permute-start.7 = (bf16[2,2,256,128]{3,2,1,0:T(8,128)(2,1)S(1)}, bf16[2,2,256,128]{3,2,1,0:T(8,128)(2,1)S(1)}, u32[]{:S(2)}, u32[]{:S(2)}) collective-permute-start(bf16[2,2,256,128]{3,2,1,0:T(8,128)(2,1)S(1)} %get-tuple-element.38), channel_id=1, source_target_pairs={{0,24},{2,26},{4,28},{6,30},{8,16},{10,18},{12,20},{14,22},{16,8},... | collective-permute-start | bytes 786440 | tf_op jit(solution)/shard_map/ppermute | solution.py:343
  52.1 10.5 %all-to-all-done.1 = bf16[16,128,128]{2,1,0:T(8,128)(2,1)S(1)} async-done(((bf16[16,128,128]{2,1,0:T(8,128)(2,1)}), bf16[16,128,128]{2,1,0:T(8,128)(2,1)S(1)}, u32[]{:S(2)}, u32[]{:S(2)}) %all-to-all-start.1) | async-done | bytes 524320 | tf_op jit(solution)/shard_map/all_to_all | solution.py:340
  62.6 16.1 %shard_map.77 = (bf16[1,1024,128]{2,1,0:T(8,128)(2,1)S(1)}, f32[1,2048,128]{2,1,0:T(8,128)S(1)}) custom-call(bf16[1,2048,128]{2,1,0:T(8,128)(2,1)S(1)} %bitcast.25, bf16[1,2048,128]{2,1,0:T(8,128)(2,1)S(1)} %bitcast.23), custom_call_target="tpu_custom_call" | custom-call | flops 10737418240 | bytes 4194304 | tf_op jit(solution)/shard_map/pallas_call | solution.py:299
  78.8 16.2 %shard_map.79 = (bf16[1,1024,128]{2,1,0:T(8,128)(2,1)S(1)}, bf16[1,2048,128]{2,1,0:T(8,128)(2,1)S(1)}, bf16[4096,1024]{1,0:T(8,128)(2,1)S(1)}, bf16[4096,1024]{1,0:T(8,128)(2,1)S(1)}) custom-call(bf16[1,2048,128]{2,1,0:T(8,128)(2,1)S(1)} %bitcast.27, bf16[1,2048,128]{2,1,0:T(8,128)(2,1)S(1)} %bitcast.24, ...), custom_call_target="tpu_custom_call" | custom-call | flops 10737418240 | bytes 4194304 | tf_op jit(solution)/shard_map/pallas_call | solution.py:299
  95.0 18.3 %all_to_all.20.refs_0_ = bf16[16,128,128]{2,1,0:T(8,128)(2,1)S(1)} all-to-all(bf16[16,128,128]{2,1,0:T(8,128)(2,1)S(1)} %bitcast.26), channel_id=1, replica_groups={{0,2,4,6,8,10,12,14,16,18,20,22,24,26,28,30},{1,3,5,7,9,11,13,15,17,19,..., dimensions={0} | all-to-all | bytes 1048576 | tf_op jit(solution)/shard_map/all_to_all | solution.py:340
  113.3 4.6 %shard_map.83 = bf16[16,64,256]{2,1,0:T(8,128)(2,1)S(1)} custom-call(bf16[16,128,128]{2,1,0:T(8,128)(2,1)S(1)} %all_to_all.20.refs_0_, bf16[4096,1024]{1,0:T(8,128)(2,1)S(1)} %get-tuple-element.42.refs_1_, bf16[4096,1024]{1,0:T(8,128)(2,1)S(1)} %get-tuple-element.43.refs_2_), custom_call_target="tpu_custom_call" | custom-call | flops 1073741824 | bytes 17301504 | tf_op jit(solution)/shard_map/pallas_call | solution.py:28
  123.6 1.8 %collective-permute-start.8 = (bf16[2,2,128,128]{3,2,1,0:T(8,128)(2,1)S(1)}, bf16[2,2,128,128]{3,2,1,0:T(8,128)(2,1)S(1)}, u32[]{:S(2)}, u32[]{:S(2)}) collective-permute-start(bf16[2,2,128,128]{3,2,1,0:T(8,128)(2,1)S(1)} %get-tuple-element.50), channel_id=1, source_target_pairs={{0,8},{2,10},{4,12},{6,14},{8,0},{10,2},{12,4},{14,6},{16,24},{18,... | collective-permute-start | bytes 393224 | tf_op jit(solution)/shard_map/ppermute | solution.py:343
  125.4 3.5 %shard_map.82.refs_1_ = f32[12,64,256]{2,1,0:T(8,128)S(1)} custom-call(bf16[16,128,128]{2,1,0:T(8,128)(2,1)S(1)} %all_to_all.20.refs_0_, bf16[4096,1024]{1,0:T(8,128)(2,1)S(1)} %get-tuple-element.42.refs_1_, bf16[4096,1024]{1,0:T(8,128)(2,1)S(1)} %get-tuple-element.43.refs_2_), custom_call_target="tpu_custom_call" | custom-call | flops 805306368 | bytes 17301504 | tf_op jit(solution)/shard_map/pallas_call | solution.py:28
  129.3 6.5 %collective-permute-done.9.refs_5_.refs_2_ = bf16[2,2,128,128]{3,2,1,0:T(8,128)(2,1)S(1)} collective-permute-done((bf16[2,2,128,128]{3,2,1,0:T(8,128)(2,1)S(1)}, bf16[2,2,128,128]{3,2,1,0:T(8,128)(2,1)S(1)}, u32[]{:S(2)}, u32[]{:S(2)}) %collective-permute-start.9) | collective-permute-done | bytes 131104 | tf_op jit(solution)/shard_map/ppermute | solution.py:343
  136.6 3.6 %all-to-all-start.3 = ((bf16[16,64,256]{2,1,0:T(8,128)(2,1)}), bf16[16,64,256]{2,1,0:T(8,128)(2,1)S(1)}, u32[]{:S(2)}, u32[]{:S(2)}) async-start(bf16[16,64,256]{2,1,0:T(8,128)(2,1)} %shard_map.84.refs_4_), calls=%async_computation.3 | async-start | bytes 1048576 | tf_op jit(solution)/shard_map/all_to_all | solution.py:420
  141.9 1.9 %collective-permute-start.13 = (bf16[4,2,128,128]{3,2,1,0:T(8,128)(2,1)S(1)}, bf16[4,2,128,128]{3,2,1,0:T(8,128)(2,1)S(1)}, u32[]{:S(2)}, u32[]{:S(2)}) collective-permute-start(bf16[4,2,128,128]{3,2,1,0:T(8,128)(2,1)S(1)} %get-tuple-element.47), channel_id=1, source_target_pairs={{0,4},{2,6},{4,0},{6,2},{8,12},{10,14},{12,8},{14,10},{16,20},{18,... | collective-permute-start | bytes 786440 | tf_op jit(solution)/shard_map/ppermute | solution.py:343
  143.8 9.7 %collective-permute-done.13.refs_2_ = bf16[4,2,128,128]{3,2,1,0:T(8,128)(2,1)S(1)} collective-permute-done((bf16[4,2,128,128]{3,2,1,0:T(8,128)(2,1)S(1)}, bf16[4,2,128,128]{3,2,1,0:T(8,128)(2,1)S(1)}, u32[]{:S(2)}, u32[]{:S(2)}) %collective-permute-start.13) | collective-permute-done | bytes 262176 | tf_op jit(solution)/shard_map/ppermute | solution.py:343
  (45 shorter events, 18.4 us)
Async XLA Ops:
  0.6 21.9 %all-to-all-start = ((bf16[16,64,256]{2,1,0:T(8,128)(2,1)}), bf16[16,64,256]{2,1,0:T(8,128)(2,1)S(1)}, u32[]{:S(2)}, u32[]{:S(2)}) async-start(bf16[16,64,256]{2,1,0:T(8,128)(2,1)} %bitcast.33), calls=%async_computation | async-start | bytes 1048576 | tf_op jit(solution)/shard_map/all_to_all | solution.py:361
  8.0 1.0 copy-start.4
  9.1 1.0 copy-start.5
  10.5 7.5 %collective-permute-start = (bf16[1,2,256,128]{3,2,1,0:T(8,128)(2,1)S(1)}, bf16[1,2,256,128]{3,2,1,0:T(8,128)(2,1)S(1)}, u32[]{:S(2)}, u32[]{:S(2)}) collective-permute-start(bf16[1,2,256,128]{3,2,1,0:T(8,128)(2,1)S(1)} %get-tuple-element.28), channel_id=1, source_target_pairs={{0,4},{2,6},{4,0},{6,2},{8,12},{10,14},{12,8},{14,10},{16,20},{18,... | collective-permute-start | bytes 393224 | tf_op jit(solution)/shard_map/ppermute | solution.py:343
  18.0 1.4 collective-permute-start.1
  22.5 15.7 %collective-permute-start.2 = (bf16[3,2,256,128]{3,2,1,0:T(8,128)(2,1)S(1)}, bf16[3,2,256,128]{3,2,1,0:T(8,128)(2,1)S(1)}, u32[]{:S(2)}, u32[]{:S(2)}) collective-permute-start(bf16[3,2,256,128]{3,2,1,0:T(8,128)(2,1)S(1)} %shard_map.71), channel_id=1, source_target_pairs={{0,4},{2,6},{4,0},{6,2},{8,12},{10,14},{12,8},{14,10},{16,20},{18,... | collective-permute-start | bytes 1179656 | tf_op jit(solution)/shard_map/ppermute | solution.py:343
  23.0 15.2 %collective-permute-start.3 = (bf16[2,2,256,128]{3,2,1,0:T(8,128)(2,1)S(1)}, bf16[2,2,256,128]{3,2,1,0:T(8,128)(2,1)S(1)}, u32[]{:S(2)}, u32[]{:S(2)}) collective-permute-start(bf16[2,2,256,128]{3,2,1,0:T(8,128)(2,1)S(1)} %shard_map.70), channel_id=1, source_target_pairs={{0,16},{2,18},{4,20},{6,22},{8,24},{10,26},{12,28},{14,30},{16,0},... | collective-permute-start | bytes 786440 | tf_op jit(solution)/shard_map/ppermute | solution.py:343
  24.9 15.2 %collective-permute-start.5 = (bf16[16,64,256]{2,1,0:T(8,128)(2,1)S(1)}, bf16[16,64,256]{2,1,0:T(8,128)(2,1)S(1)}, u32[]{:S(2)}, u32[]{:S(2)}) collective-permute-start(bf16[16,64,256]{2,1,0:T(8,128)(2,1)S(1)} %all-to-all-done.refs_1_.refs_0_), channel_id=1, source_target_pairs={{0,1},{1,0},{2,3},{3,2},{4,5},{5,4},{6,7},{7,6},{8,9},{9,8},{10,11... | collective-permute-start | bytes 1572872 | tf_op jit(solution)/shard_map/ppermute | solution.py:357
  26.4 3.4 %copy-start = (bf16[4096,1024]{1,0:T(8,128)(2,1)S(1)}, bf16[4096,1024]{1,0:T(8,128)(2,1)}, u32[]{:S(2)}) copy-start(bf16[4096,1024]{1,0:T(8,128)(2,1)} %refs_1_.7) | copy-start | bytes 25165828
  29.8 3.4 %copy-start.2 = (bf16[4096,1024]{1,0:T(8,128)(2,1)S(1)}, bf16[4096,1024]{1,0:T(8,128)(2,1)}, u32[]{:S(2)}) copy-start(bf16[4096,1024]{1,0:T(8,128)(2,1)} %refs_2_.7) | copy-start | bytes 25165828
  33.2 6.9 %copy-start.1 = (bf16[4096,1024]{1,0:T(8,128)(2,1)S(1)}, bf16[4096,1024]{1,0:T(8,128)(2,1)}, u32[]{:S(2)}) copy-start(bf16[4096,1024]{1,0:T(8,128)(2,1)} %refs_1_.7) | copy-start | bytes 25165828
  33.2 6.9 %copy-start.3 = (bf16[4096,1024]{1,0:T(8,128)(2,1)S(1)}, bf16[4096,1024]{1,0:T(8,128)(2,1)}, u32[]{:S(2)}) copy-start(bf16[4096,1024]{1,0:T(8,128)(2,1)} %refs_2_.7) | copy-start | bytes 25165828
  38.3 1.8 %collective-permute-start.4 = (bf16[3,2,256,128]{3,2,1,0:T(8,128)(2,1)S(1)}, bf16[3,2,256,128]{3,2,1,0:T(8,128)(2,1)S(1)}, u32[]{:S(2)}, u32[]{:S(2)}) collective-permute-start(bf16[3,2,256,128]{3,2,1,0:T(8,128)(2,1)S(1)} %get-tuple-element.34), channel_id=1, source_target_pairs={{0,2},{2,0},{4,6},{6,4},{8,10},{10,8},{12,14},{14,12},{16,18},{18,... | collective-permute-start | bytes 1179656 | tf_op jit(solution)/shard_map/ppermute | solution.py:343
  44.1 18.5 %all-to-all-start.1 = ((bf16[16,128,128]{2,1,0:T(8,128)(2,1)}), bf16[16,128,128]{2,1,0:T(8,128)(2,1)S(1)}, u32[]{:S(2)}, u32[]{:S(2)}) async-start(bf16[16,128,128]{2,1,0:T(8,128)(2,1)} %shard_map.76), calls=%async_computation.1 | async-start | bytes 1048576 | tf_op jit(solution)/shard_map/all_to_all | solution.py:340
  47.9 30.8 %collective-permute-start.6 = (bf16[2,2,256,128]{3,2,1,0:T(8,128)(2,1)S(1)}, bf16[2,2,256,128]{3,2,1,0:T(8,128)(2,1)S(1)}, u32[]{:S(2)}, u32[]{:S(2)}) collective-permute-start(bf16[2,2,256,128]{3,2,1,0:T(8,128)(2,1)S(1)} %get-tuple-element.37), channel_id=1, source_target_pairs={{0,8},{2,10},{4,12},{6,14},{8,0},{10,2},{12,4},{14,6},{16,24},{18,... | collective-permute-start | bytes 786440 | tf_op jit(solution)/shard_map/ppermute | solution.py:343
  49.7 29.0 %collective-permute-start.7 = (bf16[2,2,256,128]{3,2,1,0:T(8,128)(2,1)S(1)}, bf16[2,2,256,128]{3,2,1,0:T(8,128)(2,1)S(1)}, u32[]{:S(2)}, u32[]{:S(2)}) collective-permute-start(bf16[2,2,256,128]{3,2,1,0:T(8,128)(2,1)S(1)} %get-tuple-element.38), channel_id=1, source_target_pairs={{0,24},{2,26},{4,28},{6,30},{8,16},{10,18},{12,20},{14,22},{16,8},... | collective-permute-start | bytes 786440 | tf_op jit(solution)/shard_map/ppermute | solution.py:343
  117.9 17.8 %collective-permute-start.11 = (bf16[16,64,256]{2,1,0:T(8,128)(2,1)S(1)}, bf16[16,64,256]{2,1,0:T(8,128)(2,1)S(1)}, u32[]{:S(2)}, u32[]{:S(2)}) collective-permute-start(bf16[16,64,256]{2,1,0:T(8,128)(2,1)S(1)} %shard_map.83), channel_id=1, source_target_pairs={{0,1},{1,0},{2,3},{3,2},{4,5},{5,4},{6,7},{7,6},{8,9},{9,8},{10,11... | collective-permute-start | bytes 1572872 | tf_op jit(solution)/shard_map/ppermute | solution.py:357
  121.0 8.3 %collective-permute-start.10 = (bf16[2,2,128,128]{3,2,1,0:T(8,128)(2,1)S(1)}, bf16[2,2,128,128]{3,2,1,0:T(8,128)(2,1)S(1)}, u32[]{:S(2)}, u32[]{:S(2)}) collective-permute-start(bf16[2,2,128,128]{3,2,1,0:T(8,128)(2,1)S(1)} %get-tuple-element.48), channel_id=1, source_target_pairs={{0,24},{2,26},{4,28},{6,30},{8,16},{10,18},{12,20},{14,22},{16,8},... | collective-permute-start | bytes 393224 | tf_op jit(solution)/shard_map/ppermute | solution.py:343
  122.4 13.3 %collective-permute-start.9 = (bf16[2,2,128,128]{3,2,1,0:T(8,128)(2,1)S(1)}, bf16[2,2,128,128]{3,2,1,0:T(8,128)(2,1)S(1)}, u32[]{:S(2)}, u32[]{:S(2)}) collective-permute-start(bf16[2,2,128,128]{3,2,1,0:T(8,128)(2,1)S(1)} %get-tuple-element.49), channel_id=1, source_target_pairs={{0,16},{2,18},{4,20},{6,22},{8,24},{10,26},{12,28},{14,30},{16,0},... | collective-permute-start | bytes 393224 | tf_op jit(solution)/shard_map/ppermute | solution.py:343
  123.6 12.2 %collective-permute-start.8 = (bf16[2,2,128,128]{3,2,1,0:T(8,128)(2,1)S(1)}, bf16[2,2,128,128]{3,2,1,0:T(8,128)(2,1)S(1)}, u32[]{:S(2)}, u32[]{:S(2)}) collective-permute-start(bf16[2,2,128,128]{3,2,1,0:T(8,128)(2,1)S(1)} %get-tuple-element.50), channel_id=1, source_target_pairs={{0,8},{2,10},{4,12},{6,14},{8,0},{10,2},{12,4},{14,6},{16,24},{18,... | collective-permute-start | bytes 393224 | tf_op jit(solution)/shard_map/ppermute | solution.py:343
  136.6 18.0 %all-to-all-start.3 = ((bf16[16,64,256]{2,1,0:T(8,128)(2,1)}), bf16[16,64,256]{2,1,0:T(8,128)(2,1)S(1)}, u32[]{:S(2)}, u32[]{:S(2)}) async-start(bf16[16,64,256]{2,1,0:T(8,128)(2,1)} %shard_map.84.refs_4_), calls=%async_computation.3 | async-start | bytes 1048576 | tf_op jit(solution)/shard_map/all_to_all | solution.py:420
  140.3 1.6 %collective-permute-start.12 = (bf16[4,2,128,128]{3,2,1,0:T(8,128)(2,1)S(1)}, bf16[4,2,128,128]{3,2,1,0:T(8,128)(2,1)S(1)}, u32[]{:S(2)}, u32[]{:S(2)}) collective-permute-start(bf16[4,2,128,128]{3,2,1,0:T(8,128)(2,1)S(1)} %get-tuple-element.45), channel_id=1, source_target_pairs={{0,2},{2,0},{4,6},{6,4},{8,10},{10,8},{12,14},{14,12},{16,18},{18,... | collective-permute-start | bytes 786440 | tf_op jit(solution)/shard_map/ppermute | solution.py:343
  141.9 11.6 %collective-permute-start.13 = (bf16[4,2,128,128]{3,2,1,0:T(8,128)(2,1)S(1)}, bf16[4,2,128,128]{3,2,1,0:T(8,128)(2,1)S(1)}, u32[]{:S(2)}, u32[]{:S(2)}) collective-permute-start(bf16[4,2,128,128]{3,2,1,0:T(8,128)(2,1)S(1)} %get-tuple-element.47), channel_id=1, source_target_pairs={{0,4},{2,6},{4,0},{6,2},{8,12},{10,14},{12,8},{14,10},{16,20},{18,... | collective-permute-start | bytes 786440 | tf_op jit(solution)/shard_map/ppermute | solution.py:343
